TPU v7x, 32 devices: a whole 2x2x4 slice. The times are simulated.
32 devices in a mesh: role: 2 (over core), dp: 4 (over y, x), tensor: 4 (over z).
Axes of the slice: x: 2, y: 2, z: 4, core: 2. Of those that a mesh axis runs over, the one named last changes fastest.
Arguments:
- queries: bfloat16 [128, 128, 576], P(('dp', 'tensor'), 'role'), may hold values from -13 to 13
- latent_cache: bfloat16 [64, 1024, 576], P(('dp', 'tensor')), may hold values from -4 to 4
- new_latent: bfloat16 [128, 576], P(('dp', 'tensor')), may hold values from -9 to 9
- cache_lengths: int32 [64], P(('dp', 'tensor')), may hold values from 2 to 1024
- value_proj: bfloat16 [128, 512, 128], P(('role', 'tensor')), may hold values from -1 to 1
- out_proj: bfloat16 [16384, 7168], P(('role', 'tensor'), 'dp'), may hold values from -0.046875 to 0.046875
- residual: bfloat16 [128, 7168], P(('role', 'tensor'), 'dp'), may hold values from -68 to 68
- norm_gain: bfloat16 [7168], replicated, may hold values from 0.5 to 1.5
- routes: int32 [128, 8], P(('role', 'tensor')), may hold values from 0 to 15, all different within a row; in each aligned block of 16 rows (0 to 15, 16 to 31, ...) at most 10 rows name the same one
- gate_values: float32 [128, 8], P(('role', 'tensor')), may hold values from 0.2 to 0.8
- tenant_ids: int32 [128], P(('role', 'tensor')), may hold values from 0 to 2
- expert_gate_weight: bfloat16 [16, 7168, 2048], P('dp', None, ('role', 'tensor')), may hold values from -0.0625 to 0.0625
- expert_up_weight: bfloat16 [16, 7168, 2048], P('dp', None, ('role', 'tensor')), may hold values from -0.0625 to 0.0625
- expert_down_weight: bfloat16 [16, 2048, 7168], P('dp', ('role', 'tensor')), may hold values from -0.125 to 0.125
- left_delta_factor: bfloat16 [3, 16, 2048, 64], P(None, 'dp', ('role', 'tensor')), may hold values from -0.125 to 0.125
- factor_right: bfloat16 [3, 16, 64, 7168], P(None, 'dp'), may hold values from -0.75 to 0.75
Outputs:
- mixed: bfloat16 [128, 7168], P(('role', 'tensor'), 'dp')
Inputs may be any that keep to these rules, and one draw needn't show every extreme that they name: `routes`: in each aligned block of 16 tokens no expert is named by more than 10 of them.
All inputs are finite; a program needn't handle non-finite values.
Results may differ from a plain program's by a relative error of at most 0.008.
Values may be sent and summed in bfloat16 or wider, within the bound.
A program may use at most 128 MiB of HBM per device.

v0:
```python
import jax
import jax.numpy as jnp
from jax import lax
from jax.sharding import PartitionSpec as P

LAT = 512
EXPERTS = 16
TEN = 3


SCORE_SCALE = 0.07216878364870323
NORM_EPS = 1e-06
MASKED = -1e30


def rms_rows(input_rows, norm_gain):
    wide = input_rows.astype(jnp.float32)
    scale = lax.rsqrt(jnp.mean(wide * wide, axis=-1, keepdims=True) + NORM_EPS)
    return (wide * scale * norm_gain.astype(jnp.float32)).astype(jnp.bfloat16)


def local(
    queries,
    latent_cache,
    new_latent,
    cache_lengths,
    value_proj,
    out_proj,
    residual,
    norm_gain,
    routes,
    gate_values,
    tenant_ids,
    expert_gate_weight,
    expert_up_weight,
    expert_down_weight,
    left_delta_factor,
    factor_right,
):
    seq_count, context, width = latent_cache.shape
    local_heads = queries.shape[1]
    paired = queries.reshape(seq_count, 2, local_heads, width)
    scores = (
        jnp.einsum("sqhd,spd->sqhp", paired, latent_cache, preferred_element_type=jnp.float32)
        * SCORE_SCALE
    )
    present = jnp.arange(context, dtype=jnp.int32)[None, :] < cache_lengths[:, None]
    scores = jnp.where(present[:, None, None, :], scores, MASKED)
    fresh_keys = new_latent.reshape(seq_count, 2, width)
    fresh = (
        jnp.einsum("sqhd,skd->sqhk", paired, fresh_keys, preferred_element_type=jnp.float32)
        * SCORE_SCALE
    )
    causal = jnp.arange(2)[:, None] >= jnp.arange(2)[None, :]
    fresh = jnp.where(causal[None, :, None, :], fresh, MASKED)
    top = jnp.maximum(jnp.max(scores, axis=3), jnp.max(fresh, axis=3))[..., None]
    weights = jnp.exp(scores - top)
    fresh_weights = jnp.exp(fresh - top)
    total = jnp.sum(weights, axis=3) + jnp.sum(fresh_weights, axis=3)
    summed = jnp.einsum(
        "sqhp,spd->sqhd",
        weights.astype(jnp.bfloat16),
        latent_cache[:, :, :LAT],
        preferred_element_type=jnp.float32,
    )
    summed = summed + jnp.einsum(
        "sqhk,skd->sqhd",
        fresh_weights.astype(jnp.bfloat16),
        fresh_keys[:, :, :LAT],
        preferred_element_type=jnp.float32,
    )
    attended = (
        (summed / total[..., None]).astype(jnp.bfloat16).reshape(seq_count * 2, local_heads, LAT)
    )
    by_head = lax.all_to_all(attended, "tensor", split_axis=1, concat_axis=0, tiled=True)
    head_values = jnp.einsum(
        "thl,hlv->thv", by_head, value_proj, preferred_element_type=jnp.float32
    ).astype(jnp.bfloat16)
    head_values = head_values.reshape(
        head_values.shape[0], head_values.shape[1] * head_values.shape[2]
    )
    all_values = lax.all_gather(head_values, "dp", axis=0, tiled=True)
    group_rows = residual.shape[0]
    input_rows = all_values
    attention = lax.psum_scatter(
        jnp.dot(input_rows, out_proj, preferred_element_type=jnp.float32),
        ("role", "tensor"),
        scatter_dimension=0,
        tiled=True,
    )
    mixed_in = lax.optimization_barrier(
        (residual.astype(jnp.float32) + attention).astype(jnp.bfloat16)
    )
    capacity = 5 * group_rows // 8
    labels = jnp.arange(EXPERTS, dtype=jnp.int32)
    chosen = (routes[:, :, None] == labels[None, None, :]).astype(jnp.int32)
    routed = jnp.sum(chosen, axis=1)
    earlier = jnp.cumsum(routed, axis=0) - routed
    slot_ids = jnp.arange(capacity, dtype=jnp.int32)
    table = (routed.T[:, None, :] > 0) & (earlier.T[:, None, :] == slot_ids[None, :, None])
    local_experts = EXPERTS // lax.axis_size("dp")
    expert_start = lax.axis_index("dp") * local_experts
    mine = lax.dynamic_slice_in_dim(table, expert_start, local_experts, 0)
    full_rows = lax.all_gather(mixed_in, "dp", axis=1, tiled=True)
    picked = jnp.einsum(
        "ecg,gd->ecd", mine.astype(jnp.bfloat16), full_rows, preferred_element_type=jnp.float32
    ).astype(jnp.bfloat16)
    slot_rows = rms_rows(picked, norm_gain)
    slot_owner = jnp.sum(mine.astype(jnp.int32) * tenant_ids[None, None, :], axis=2)
    collected_rows, owners = (
        lax.all_gather(slot_rows, ("role", "tensor"), axis=1, tiled=True),
        lax.all_gather(slot_owner, ("role", "tensor"), axis=1, tiled=True),
    )
    gate_scores = jnp.einsum(
        "gpc,gcb->gpb", collected_rows, expert_gate_weight, preferred_element_type=jnp.float32
    )
    upper_bound = jnp.einsum(
        "gpc,gcb->gpb", collected_rows, expert_up_weight, preferred_element_type=jnp.float32
    )
    hidden = (jax.nn.silu(gate_scores) * upper_bound).astype(jnp.bfloat16)
    owner_mask = (owners[:, :, None] == jnp.arange(TEN, dtype=jnp.int32)[None, None, :]).astype(
        jnp.float32
    )
    widened_right_factor = factor_right.astype(jnp.float32)
    input_rows = hidden
    base_output = jnp.einsum(
        "xog,xgm->oxm", input_rows, expert_down_weight, preferred_element_type=jnp.float32
    )
    mixing_coefficient = (
        jnp.einsum(
            "ywv,oyvh->ywoh", input_rows, left_delta_factor, preferred_element_type=jnp.float32
        )
        * owner_mask[..., None]
    )
    outputs = lax.psum_scatter(
        base_output
        - jnp.einsum(
            "okei,eoiw->kow",
            mixing_coefficient,
            widened_right_factor,
            precision=lax.Precision.HIGHEST,
        ),
        ("role", "tensor"),
        scatter_dimension=0,
        tiled=True,
    ).astype(jnp.bfloat16)
    gate_of = jnp.sum(gate_values[:, :, None] * chosen.astype(jnp.float32), axis=1)
    weighting = table.astype(jnp.float32) * gate_of.T[:, None, :]
    own_weights = lax.dynamic_slice_in_dim(weighting, expert_start, local_experts, 0)
    token_terms = jnp.einsum(
        "lcg,cld->gd", own_weights, outputs.astype(jnp.float32), precision=lax.Precision.HIGHEST
    )
    expert_part = lax.psum_scatter(token_terms, "dp", scatter_dimension=1, tiled=True)
    return (mixed_in.astype(jnp.float32) + expert_part).astype(jnp.bfloat16)


def solution(mesh):
    placed = (
        P(("dp", "tensor"), "role", None),
        P(("dp", "tensor"), None, None),
        P(("dp", "tensor"), None),
        P(("dp", "tensor")),
        P(("role", "tensor"), None, None),
        P(("role", "tensor"), "dp"),
        P(("role", "tensor"), "dp"),
        P(),
        P(("role", "tensor"), None),
        P(("role", "tensor"), None),
        P(("role", "tensor")),
        P("dp", None, ("role", "tensor")),
        P("dp", None, ("role", "tensor")),
        P("dp", ("role", "tensor"), None),
        P(None, "dp", ("role", "tensor"), None),
        P(None, "dp", None, None),
    )
    return jax.shard_map(
        local, mesh=mesh, in_specs=placed, out_specs=P(("role", "tensor"), "dp"), check_vma=False
    )
```

profile of v0, /device:TPU:0, one launch (start us, length us, event | category | flops | bytes accessed | tf_op | source)
XLA Modules:
  0.0 590.6 jit_solution(15686372871514538455)
XLA Ops:
  6.5 0.9 reshape.79
  7.4 0.7 reshape.73
  8.1 0.7 iota_compare_fusion.2
  8.9 1.7 fusion.59
  10.5 0.0 slice-start.3
  10.5 3.8 fusion.16
  14.4 0.6 fusion.17
  15.0 1.7 fusion.9
  16.8 0.4 fusion.20
  17.2 0.3 copy.51
  17.5 20.6 %all_to_all.18 = bf16[8,64,512]{2,0,1:T(8,128)(2,1)S(1)} all-to-all(bf16[8,64,512]{2,0,1:T(8,128)(2,1)S(1)} %copy.51), channel_id=1, replica_groups=mesh['role'=2,'dp'=4,'tensor'=4] {'tensor'}, dimensions={1} | all-to-all | bytes 1048576 | tf_op jit(solution)/shard_map/all_to_all | solution.py:75
  38.1 0.4 fusion.27
  38.5 10.2 %all_gather.12 = bf16[128,2048]{1,0:T(8,128)(2,1)S(1)} all-gather(bf16[32,2048]{1,0:T(8,128)(2,1)S(1)} %bitcast.83), channel_id=1, replica_groups=mesh['role'=2,'dp'=4,'tensor'=4] {'dp'}, dimensions={0}, use_global_device_ids=true | all-gather | bytes 655360 | tf_op jit(solution)/shard_map/all_gather | solution.py:82
  48.8 2.1 fusion.60
  50.9 0.0 reduce-scatter.3.cloned.1.call-update
  50.9 0.0 all-gather.3.cloned.1.call-start
  51.0 0.1 copy.54
  51.0 0.1 convert_reduce_fusion
  51.2 0.1 copy.55
  51.3 0.1 copy.56
  51.4 33.0 %reduce-scatter.3.cloned.1.call-done = f32[16,1792]{1,0:T(8,128)} async-done(((f32[128,1792]{1,0:T(8,128)}), f32[16,1792]{1,0:T(8,128)}) %reduce-scatter.3.cloned.1.call-update) | async-done | bytes 114704 | tf_op jit(solution)/shard_map/reduce_scatter | solution.py:85
  84.4 0.9 add_convert_fusion.1
  85.3 8.9 %all_gather.13 = bf16[16,7168]{1,0:T(8,128)(2,1)S(1)} all-gather(bf16[16,1792]{1,0:T(8,128)(2,1)S(1)} %add_convert_fusion.1), channel_id=1, replica_groups=mesh['role'=2,'dp'=4,'tensor'=4] {'dp'}, dimensions={1}, use_global_device_ids=true | all-gather | bytes 286720 | tf_op jit(solution)/shard_map/all_gather | solution.py:104
  94.2 0.5 multiply_reduce_fusion
  94.7 0.2 multiply_convert_fusion
  94.9 1.3 copy.59
  96.2 0.0 all-gather.3.cloned.1.call-update
  96.2 0.0 reduce-scatter.5.cloned.1.call-start
  96.3 0.1 copy.57
  96.4 0.1 fusion.42
  96.5 0.1 copy.58
  96.5 0.1 select_reduce_fusion
  96.7 22.2 %all-gather = s32[8,10,4]{1,2,0:T(4,128)S(1)} all-gather(s32[1,10,4]{1,2,0:T(4,128)S(1)} %bitcast.87), channel_id=1, replica_groups=mesh['role'=2,'dp'=4,'tensor'=4] {'role','tensor'}, dimensions={0}, use_global_device_ids=true | all-gather | bytes 1440 | tf_op jit(solution)/shard_map/all_gather | solution.py:112
  118.9 0.1 reshape.77
  119.0 0.6 dynamic-slice
  120.2 24.8 %all-gather.3.cloned.1.call-done = bf16[4,80,7168]{2,0,1:T(4,128)(2,1)} async-done(((bf16[4,10,7168]{2,0,1:T(4,128)(2,1)}), bf16[4,80,7168]{2,0,1:T(4,128)(2,1)}) %all-gather.3.cloned.1.call-update) | async-done | bytes 4587536 | tf_op jit(solution)/shard_map/all_gather | solution.py:111
  145.0 9.2 %fusion.14 = f32[4,80,256]{2,1,0:T(8,128)S(1)} fusion(bf16[4,7168,256]{2,1,0:T(8,128)(2,1)} %param.27, bf16[4,80,7168]{2,0,1:T(4,128)(2,1)} %all-gather.3.cloned.1.call-done), kind=kOutput, calls=%fused_computation.15 | convolution fusion | flops 1174405120 | bytes 19595264 | tf_op jit(solution)/shard_map/gpc,gcb->gpb/dot_general | solution.py:114
  154.2 7.7 %fusion.24 = bf16[4,80,256]{2,1,0:T(8,128)(2,1)S(1)} fusion(bf16[4,7168,256]{2,1,0:T(8,128)(2,1)} %param.28, bf16[4,80,7168]{2,0,1:T(4,128)(2,1)S(1)} %copy-done.2, f32[4,80,256]{2,1,0:T(8,128)S(1)} %fusion.14), kind=kOutput, calls=%fused_computation.29 | convolution fusion | flops 1174896640 | bytes 19759104 | tf_op jit(solution)/shard_map/gpc,gcb->gpb/dot_general | solution.py:117
  162.0 0.2 convolution_multiply_fusion
  162.2 9.1 %fusion.3 = f32[4,80,7168]{2,1,0:T(8,128)S(1)} fusion(f32[4,80,3,64]{1,3,2,0:T(8,128)S(1)} %convolution_multiply_fusion, bf16[3,4,64,7168]{3,2,1,0:T(8,128)(2,1)} %param.31), kind=kOutput, calls=%fused_computation.4 | convolution fusion | flops 5284823040 | bytes 20430848 | tf_op jit(solution)/shard_map/okei,eoiw->kow/dot_general | solution.py:137
  171.3 11.7 %fusion.2 = f32[80,4,7168]{2,0,1:T(8,128)} fusion(f32[4,80,7168]{2,1,0:T(8,128)S(1)} %fusion.3, bf16[4,80,256]{2,1,0:T(8,128)(2,1)S(1)} %fusion.24, bf16[4,256,7168]{2,1,0:T(8,128)(2,1)} %param.29), kind=kOutput, calls=%fused_computation.3 | convolution fusion | flops 1176698880 | bytes 33193984 | tf_op jit(solution)/shard_map/xog,xgm->oxm/dot_general | solution.py:126
  183.0 13.0 %copy.65 = f32[80,4,7168]{2,1,0:T(4,128)} copy(f32[80,4,7168]{2,0,1:T(8,128)} %fusion.2) | data formatting | bytes 18350080 | tf_op jit(solution)/shard_map/sub | solution.py:136
  196.0 357.2 %all-reduce.2 = bf16[80,4,7168]{2,1,0:T(4,128)(2,1)} all-reduce(f32[80,4,7168]{2,1,0:T(4,128)} %copy.65), channel_id=3, replica_groups=mesh['role'=2,'dp'=4,'tensor'=4] {'role','tensor'}, use_global_device_ids=true, to_apply=%region_10.11.clone | all-reduce | flops 2293760 | bytes 13762560
  553.3 1.3 dynamic-slice_convert_fusion
  554.5 1.4 convolution_bitcast_fusion
  555.9 0.0 reduce-scatter.5.cloned.1.call-update
  555.9 26.6 %reduce-scatter.5.cloned.1.call-done = f32[16,1792]{1,0:T(8,128)} async-done(((f32[16,7168]{1,0:T(8,128)}), f32[16,1792]{1,0:T(8,128)}) %reduce-scatter.5.cloned.1.call-update) | async-done | bytes 114704 | tf_op jit(solution)/shard_map/reduce_scatter | solution.py:153
  582.5 1.5 add_convert_fusion
  (44 shorter events, 0.2 us)
Async XLA Ops:
  6.5 31.5 %copy-start = (bf16[16,512,128]{2,1,0:T(8,128)(2,1)S(1)}, bf16[16,512,128]{2,1,0:T(8,128)(2,1)}, u32[]{:S(2)}) copy-start(bf16[16,512,128]{2,1,0:T(8,128)(2,1)} %param.20) | copy-start | bytes 6291460
  6.5 77.9 %reduce-scatter.3.cloned.1.call-start = ((), (), s32[]{:S(2)}) async-start(), calls=%async_computation.3 | async-start | bytes 1032192 | tf_op jit(solution)/shard_map/reduce_scatter | solution.py:85
  8.9 6.1 %slice-start.2 = ((s8[4718592]{0:T(1024)(128)(4,1)}), s8[4194304]{0:T(1024)(128)(4,1)S(1)}, s32[]{:S(2)}) async-start(s8[4718592]{0:T(1024)(128)(4,1)} %bitcast.78), calls=%async_computation.8 | async-start | bytes 8388608
  10.5 4.5 slice-start.3
  14.4 34.4 %slice-start = ((s8[7340032]{0:T(1024)(128)(4,1)}), s8[4194304]{0:T(1024)(128)(4,1)S(1)}, s32[]{:S(2)}) async-start(s8[7340032]{0:T(1024)(128)(4,1)} %bitcast.76), calls=%async_computation.6 | async-start | bytes 8388608
  15.0 33.7 %slice-start.1 = ((s8[7340032]{0:T(1024)(128)(4,1)}), s8[3145728]{0:T(1024)(128)(4,1)S(1)}, s32[]{:S(2)}) async-start(s8[7340032]{0:T(1024)(128)(4,1)} %bitcast.76), calls=%async_computation.7 | async-start | bytes 6291456
  48.8 2.2 copy-start.6
  48.8 2.6 copy-start.5
  48.8 35.6 %copy-start.4 = (bf16[16,1792]{1,0:T(8,128)(2,1)S(1)}, bf16[16,1792]{1,0:T(8,128)(2,1)}, u32[]{:S(2)}) copy-start(bf16[16,1792]{1,0:T(8,128)(2,1)} %param.22) | copy-start | bytes 172036
  50.9 45.4 %copy-start.7 = (f32[16,8]{0,1:T(8,128)S(1)}, f32[16,8]{0,1:T(8,128)}, u32[]{:S(2)}) copy-start(f32[16,8]{0,1:T(8,128)} %param.25) | copy-start | bytes 1540
  50.9 45.7 %copy-start.8 = (s32[16]{0:T(128)S(1)}, s32[16]{0:T(128)}, u32[]{:S(2)}) copy-start(s32[16]{0:T(128)} %param.26) | copy-start | bytes 196
  50.9 68.1 %copy-start.9 = (u32[32]{0:T(128)S(1)}, u32[32]{0:T(128)}, u32[]{:S(2)}) copy-start(u32[32]{0:T(128)} %constant.40) | copy-start | bytes 388
  50.9 94.1 %all-gather.3.cloned.1.call-start = ((), (), s32[]{:S(2)}) async-start(), calls=%async_computation.4 | async-start | bytes 5160960 | tf_op jit(solution)/shard_map/all_gather | solution.py:111
  96.2 486.3 %reduce-scatter.5.cloned.1.call-start = ((), (), s32[]{:S(2)}) async-start(), calls=%async_computation.5 | async-start | bytes 573440 | tf_op jit(solution)/shard_map/reduce_scatter | solution.py:153
  145.0 9.2 %copy-start.2 = (bf16[4,80,7168]{2,0,1:T(4,128)(2,1)S(1)}, bf16[4,80,7168]{2,0,1:T(4,128)(2,1)}, u32[]{:S(2)}) copy-start(bf16[4,80,7168]{2,0,1:T(4,128)(2,1)} %all-gather.3.cloned.1.call-done) | copy-start | bytes 13762564
  154.2 7.8 %copy-start.3 = (bf16[3,4,256,64]{2,3,1,0:T(8,128)(2,1)S(1)}, bf16[3,4,256,64]{2,3,1,0:T(8,128)(2,1)}, u32[]{:S(2)}) copy-start(bf16[3,4,256,64]{2,3,1,0:T(8,128)(2,1)} %param.30) | copy-start | bytes 1179652
  196.0 388.0 %copy-start.1 = (bf16[16,512,128]{2,1,0:T(8,128)(2,1)S(1)}, bf16[16,512,128]{2,1,0:T(8,128)(2,1)}, u32[]{:S(2)}) copy-start(bf16[16,512,128]{2,1,0:T(8,128)(2,1)} %param.20) | copy-start | bytes 6291460
Sparse Core Ops, SparseCore 0:
  51.0 33.3 reduce-scatter.2
  96.3 48.6 all-gather.2
  556.0 26.4 reduce-scatter.4
where the time goes:
time: 591 us
  blocking collectives  419 us (71%)
  waiting for transfers between devices  84.4 us (14%)
  matrix products  49.8 us (8%)
  local copies, waits for them, and re-layouts  18.6 us (3%)
  between operations  14.1 us (2%)
    unnamed x1, blocking collectives  357 us
    reduce_scatter x1, waiting for transfers between devices, local(): lax.psum_scatter(jnp.dot(input_rows, out_proj, preferred_element_type=jnp...  33 us
    reduce_scatter x1, waiting for transfers between devices, local(): lax.psum_scatter(token_terms, 'dp', scatter_dimension=1, tiled=True)  26.6 us
    all_gather x1, waiting for transfers between devices, local(): lax.all_gather(slot_rows, ('role', 'tensor'), axis=1, tiled=True)  24.8 us
    all_gather x1, blocking collectives, local(): lax.all_gather(slot_owner, ('role', 'tensor'), axis=1, tiled=True)  22.2 us
    all_to_all x1, blocking collectives, local(): lax.all_to_all(attended, 'tensor', split_axis=1, concat_axis=0, tiled=True)  20.6 us
    sub x1, local copies, waits for them, and re-layouts, local(): base_output - jnp.einsum('okei,eoiw->kow', mixing_coefficient, widened_ri...  13 us
  transfers between devices with their start and end apart: 3, of which 3 were waited for; matrix products, arithmetic and copies ran while one was open for 0% of the time, Pallas kernels for 0%

commit v1 on v0

--- a/solution.py
+++ b/solution.py
@@ -95,7 +95,9 @@
     labels = jnp.arange(EXPERTS, dtype=jnp.int32)
     chosen = (routes[:, :, None] == labels[None, None, :]).astype(jnp.int32)
     routed = jnp.sum(chosen, axis=1)
-    earlier = jnp.cumsum(routed, axis=0) - routed
+    rows_at = jnp.arange(group_rows, dtype=jnp.int32)
+    before = (rows_at[:, None] > rows_at[None, :]).astype(jnp.int32)
+    earlier = jnp.sum(before[:, :, None] * routed[None, :, :], axis=1)
     slot_ids = jnp.arange(capacity, dtype=jnp.int32)
     table = (routed.T[:, None, :] > 0) & (earlier.T[:, None, :] == slot_ids[None, :, None])
     local_experts = EXPERTS // lax.axis_size("dp")

time: 591 us -> 591 us (level)
  no operation moved by 1% of the time
where the time goes in v1:
time: 591 us
  blocking collectives  419 us (71%)
  waiting for transfers between devices  84.3 us (14%)
  matrix products  49.8 us (8%)
  local copies, waits for them, and re-layouts  18.6 us (3%)
  between operations  14.1 us (2%)
    unnamed x1, blocking collectives  357 us
    reduce_scatter x1, waiting for transfers between devices, local(): lax.psum_scatter(jnp.dot(input_rows, out_proj, preferred_element_type=jnp...  32.9 us
    reduce_scatter x1, waiting for transfers between devices, local(): lax.psum_scatter(token_terms, 'dp', scatter_dimension=1, tiled=True)  26.6 us
    all_gather x1, waiting for transfers between devices, local(): lax.all_gather(slot_rows, ('role', 'tensor'), axis=1, tiled=True)  24.8 us
    all_gather x1, blocking collectives, local(): lax.all_gather(slot_owner, ('role', 'tensor'), axis=1, tiled=True)  22.2 us
    all_to_all x1, blocking collectives, local(): lax.all_to_all(attended, 'tensor', split_axis=1, concat_axis=0, tiled=True)  20.6 us
    sub x1, local copies, waits for them, and re-layouts, local(): base_output - jnp.einsum('okei,eoiw->kow', mixing_coefficient, widened_ri...  13 us
  transfers between devices with their start and end apart: 3, of which 3 were waited for; matrix products, arithmetic and copies ran while one was open for 0% of the time, Pallas kernels for 0%

profile of v1, /device:TPU:0, one launch (start us, length us, event | category | flops | bytes accessed | tf_op | source)
XLA Modules:
  0.0 590.6 jit_solution(17902700071741361181)
XLA Ops:
  6.5 0.9 reshape.93
  7.4 0.7 reshape.87
  8.1 0.7 iota_compare_fusion.2
  8.9 1.7 fusion.60
  10.5 3.8 fusion.16
  14.4 0.6 fusion.17
  15.0 1.7 fusion.9
  16.8 0.4 fusion.20
  17.2 0.3 copy.48
  17.5 20.6 %all_to_all.18 = bf16[8,64,512]{2,0,1:T(8,128)(2,1)S(1)} all-to-all(bf16[8,64,512]{2,0,1:T(8,128)(2,1)S(1)} %copy.48), channel_id=1, replica_groups=mesh['role'=2,'dp'=4,'tensor'=4] {'tensor'}, dimensions={1} | all-to-all | bytes 1048576 | tf_op jit(solution)/shard_map/all_to_all | solution.py:75
  38.1 0.4 fusion.27
  38.5 10.2 %all_gather.12 = bf16[128,2048]{1,0:T(8,128)(2,1)S(1)} all-gather(bf16[32,2048]{1,0:T(8,128)(2,1)S(1)} %bitcast.82), channel_id=1, replica_groups=mesh['role'=2,'dp'=4,'tensor'=4] {'dp'}, dimensions={0}, use_global_device_ids=true | all-gather | bytes 655360 | tf_op jit(solution)/shard_map/all_gather | solution.py:82
  48.8 2.1 fusion.61
  50.9 0.0 reduce-scatter.3.cloned.1.call-update
  50.9 0.0 all-gather.3.cloned.1.call-start
  51.0 0.1 copy.51
  51.0 0.1 convert_reduce_fusion
  51.2 0.1 copy.52
  51.3 0.1 multiply_reduce_fusion.1
  51.4 0.1 copy.53
  51.5 32.9 %reduce-scatter.3.cloned.1.call-done = f32[16,1792]{1,0:T(8,128)} async-done(((f32[128,1792]{1,0:T(8,128)}), f32[16,1792]{1,0:T(8,128)}) %reduce-scatter.3.cloned.1.call-update) | async-done | bytes 114704 | tf_op jit(solution)/shard_map/reduce_scatter | solution.py:85
  84.4 0.9 add_convert_fusion.1
  85.3 8.9 %all_gather.13 = bf16[16,7168]{1,0:T(8,128)(2,1)S(1)} all-gather(bf16[16,1792]{1,0:T(8,128)(2,1)S(1)} %add_convert_fusion.1), channel_id=1, replica_groups=mesh['role'=2,'dp'=4,'tensor'=4] {'dp'}, dimensions={1}, use_global_device_ids=true | all-gather | bytes 286720 | tf_op jit(solution)/shard_map/all_gather | solution.py:106
  94.2 0.5 multiply_reduce_fusion
  94.7 0.2 multiply_convert_fusion
  94.9 1.3 copy.56
  96.2 0.0 all-gather.3.cloned.1.call-update
  96.2 0.0 reduce-scatter.5.cloned.1.call-start
  96.3 0.1 copy.54
  96.4 0.1 fusion.42
  96.5 0.1 copy.55
  96.5 0.1 select_reduce_fusion
  96.7 22.2 %all-gather = s32[8,10,4]{1,2,0:T(4,128)S(1)} all-gather(s32[1,10,4]{1,2,0:T(4,128)S(1)} %bitcast.87), channel_id=1, replica_groups=mesh['role'=2,'dp'=4,'tensor'=4] {'role','tensor'}, dimensions={0}, use_global_device_ids=true | all-gather | bytes 1440 | tf_op jit(solution)/shard_map/all_gather | solution.py:114
  118.9 0.1 reshape.91
  119.0 0.6 dynamic-slice
  120.2 24.8 %all-gather.3.cloned.1.call-done = bf16[4,80,7168]{2,0,1:T(4,128)(2,1)} async-done(((bf16[4,10,7168]{2,0,1:T(4,128)(2,1)}), bf16[4,80,7168]{2,0,1:T(4,128)(2,1)}) %all-gather.3.cloned.1.call-update) | async-done | bytes 4587536 | tf_op jit(solution)/shard_map/all_gather | solution.py:113
  145.0 9.2 %fusion.14 = f32[4,80,256]{2,1,0:T(8,128)S(1)} fusion(bf16[4,7168,256]{2,1,0:T(8,128)(2,1)} %param.27, bf16[4,80,7168]{2,0,1:T(4,128)(2,1)} %all-gather.3.cloned.1.call-done), kind=kOutput, calls=%fused_computation.15 | convolution fusion | flops 1174405120 | bytes 19595264 | tf_op jit(solution)/shard_map/gpc,gcb->gpb/dot_general | solution.py:116
  154.2 7.7 %fusion.24 = bf16[4,80,256]{2,1,0:T(8,128)(2,1)S(1)} fusion(bf16[4,7168,256]{2,1,0:T(8,128)(2,1)} %param.28, bf16[4,80,7168]{2,0,1:T(4,128)(2,1)S(1)} %copy-done.2, f32[4,80,256]{2,1,0:T(8,128)S(1)} %fusion.14), kind=kOutput, calls=%fused_computation.29 | convolution fusion | flops 1174896640 | bytes 19759104 | tf_op jit(solution)/shard_map/gpc,gcb->gpb/dot_general | solution.py:119
  162.0 0.2 convolution_multiply_fusion
  162.2 9.1 %fusion.3 = f32[4,80,7168]{2,1,0:T(8,128)S(1)} fusion(f32[4,80,3,64]{1,3,2,0:T(8,128)S(1)} %convolution_multiply_fusion, bf16[3,4,64,7168]{3,2,1,0:T(8,128)(2,1)} %param.31), kind=kOutput, calls=%fused_computation.4 | convolution fusion | flops 5284823040 | bytes 20430848 | tf_op jit(solution)/shard_map/okei,eoiw->kow/dot_general | solution.py:139
  171.3 11.7 %fusion.2 = f32[80,4,7168]{2,0,1:T(8,128)} fusion(f32[4,80,7168]{2,1,0:T(8,128)S(1)} %fusion.3, bf16[4,80,256]{2,1,0:T(8,128)(2,1)S(1)} %fusion.24, bf16[4,256,7168]{2,1,0:T(8,128)(2,1)} %param.29), kind=kOutput, calls=%fused_computation.3 | convolution fusion | flops 1176698880 | bytes 33193984 | tf_op jit(solution)/shard_map/xog,xgm->oxm/dot_general | solution.py:128
  183.0 13.0 %copy.62 = f32[80,4,7168]{2,1,0:T(4,128)} copy(f32[80,4,7168]{2,0,1:T(8,128)} %fusion.2) | data formatting | bytes 18350080 | tf_op jit(solution)/shard_map/sub | solution.py:138
  196.0 357.2 %all-reduce.2 = bf16[80,4,7168]{2,1,0:T(4,128)(2,1)} all-reduce(f32[80,4,7168]{2,1,0:T(4,128)} %copy.62), channel_id=3, replica_groups=mesh['role'=2,'dp'=4,'tensor'=4] {'role','tensor'}, use_global_device_ids=true, to_apply=%region_10.11.clone | all-reduce | flops 2293760 | bytes 13762560
  553.3 1.3 dynamic-slice_convert_fusion
  554.5 1.4 convolution_bitcast_fusion
  555.9 0.0 reduce-scatter.5.cloned.1.call-update
  555.9 26.6 %reduce-scatter.5.cloned.1.call-done = f32[16,1792]{1,0:T(8,128)} async-done(((f32[16,7168]{1,0:T(8,128)}), f32[16,1792]{1,0:T(8,128)}) %reduce-scatter.5.cloned.1.call-update) | async-done | bytes 114704 | tf_op jit(solution)/shard_map/reduce_scatter | solution.py:155
  582.5 1.5 add_convert_fusion
  (44 shorter events, 0.2 us)
Async XLA Ops:
  6.5 31.5 %copy-start = (bf16[16,512,128]{2,1,0:T(8,128)(2,1)S(1)}, bf16[16,512,128]{2,1,0:T(8,128)(2,1)}, u32[]{:S(2)}) copy-start(bf16[16,512,128]{2,1,0:T(8,128)(2,1)} %param.20) | copy-start | bytes 6291460
  6.5 77.9 %reduce-scatter.3.cloned.1.call-start = ((), (), s32[]{:S(2)}) async-start(), calls=%async_computation.3 | async-start | bytes 1032192 | tf_op jit(solution)/shard_map/reduce_scatter | solution.py:85
  8.9 6.1 %slice-start.2 = ((s8[4718592]{0:T(1024)(128)(4,1)}), s8[4194304]{0:T(1024)(128)(4,1)S(1)}, s32[]{:S(2)}) async-start(s8[4718592]{0:T(1024)(128)(4,1)} %bitcast.77), calls=%async_computation.8 | async-start | bytes 8388608
  10.5 4.5 slice-start.3
  14.4 34.4 %slice-start = ((s8[7340032]{0:T(1024)(128)(4,1)}), s8[4194304]{0:T(1024)(128)(4,1)S(1)}, s32[]{:S(2)}) async-start(s8[7340032]{0:T(1024)(128)(4,1)} %bitcast.75), calls=%async_computation.6 | async-start | bytes 8388608
  15.0 33.7 %slice-start.1 = ((s8[7340032]{0:T(1024)(128)(4,1)}), s8[3145728]{0:T(1024)(128)(4,1)S(1)}, s32[]{:S(2)}) async-start(s8[7340032]{0:T(1024)(128)(4,1)} %bitcast.75), calls=%async_computation.7 | async-start | bytes 6291456
  48.8 2.2 copy-start.6
  48.8 2.7 copy-start.5
  48.8 35.6 %copy-start.4 = (bf16[16,1792]{1,0:T(8,128)(2,1)S(1)}, bf16[16,1792]{1,0:T(8,128)(2,1)}, u32[]{:S(2)}) copy-start(bf16[16,1792]{1,0:T(8,128)(2,1)} %param.22) | copy-start | bytes 172036
  50.9 45.4 %copy-start.7 = (f32[16,8]{0,1:T(8,128)S(1)}, f32[16,8]{0,1:T(8,128)}, u32[]{:S(2)}) copy-start(f32[16,8]{0,1:T(8,128)} %param.25) | copy-start | bytes 1540
  50.9 45.7 %copy-start.8 = (s32[16]{0:T(128)S(1)}, s32[16]{0:T(128)}, u32[]{:S(2)}) copy-start(s32[16]{0:T(128)} %param.26) | copy-start | bytes 196
  50.9 68.1 %copy-start.9 = (u32[32]{0:T(128)S(1)}, u32[32]{0:T(128)}, u32[]{:S(2)}) copy-start(u32[32]{0:T(128)} %constant.37) | copy-start | bytes 388
  50.9 94.1 %all-gather.3.cloned.1.call-start = ((), (), s32[]{:S(2)}) async-start(), calls=%async_computation.4 | async-start | bytes 5160960 | tf_op jit(solution)/shard_map/all_gather | solution.py:113
  96.2 486.3 %reduce-scatter.5.cloned.1.call-start = ((), (), s32[]{:S(2)}) async-start(), calls=%async_computation.5 | async-start | bytes 573440 | tf_op jit(solution)/shard_map/reduce_scatter | solution.py:155
  145.0 9.2 %copy-start.2 = (bf16[4,80,7168]{2,0,1:T(4,128)(2,1)S(1)}, bf16[4,80,7168]{2,0,1:T(4,128)(2,1)}, u32[]{:S(2)}) copy-start(bf16[4,80,7168]{2,0,1:T(4,128)(2,1)} %all-gather.3.cloned.1.call-done) | copy-start | bytes 13762564
  154.2 7.8 %copy-start.3 = (bf16[3,4,256,64]{2,3,1,0:T(8,128)(2,1)S(1)}, bf16[3,4,256,64]{2,3,1,0:T(8,128)(2,1)}, u32[]{:S(2)}) copy-start(bf16[3,4,256,64]{2,3,1,0:T(8,128)(2,1)} %param.30) | copy-start | bytes 1179652
  196.0 388.0 %copy-start.1 = (bf16[16,512,128]{2,1,0:T(8,128)(2,1)S(1)}, bf16[16,512,128]{2,1,0:T(8,128)(2,1)}, u32[]{:S(2)}) copy-start(bf16[16,512,128]{2,1,0:T(8,128)(2,1)} %param.20) | copy-start | bytes 6291460
Sparse Core Ops, SparseCore 0:
  51.0 33.3 reduce-scatter.2
  96.3 48.6 all-gather.2
  556.0 26.4 reduce-scatter.4

commit v2 on v0

v2 whole, which is shorter than its diff:
```python
import functools
import jax
import jax.numpy as jnp
from jax import lax
from jax.experimental import pallas as pl
from jax.experimental.pallas import tpu as pltpu
from jax.sharding import PartitionSpec as P

LAT = 512
EXPERTS = 16
TEN = 3


SCORE_SCALE = 0.07216878364870323
NORM_EPS = 1e-06
MASKED = -1e30


MESH = pl.DeviceIdType.MESH
VMEM_BYTES = 56 * 1024 * 1024


def peer_of(axis, offset):
    size = lax.axis_size(axis)
    return lax.rem(lax.axis_index(axis) + offset, size)


def source_of(axis, offset):
    size = lax.axis_size(axis)
    return lax.rem(lax.axis_index(axis) + size - offset, size)


def greet(axes):
    barrier = pltpu.get_barrier_semaphore()
    count = 0
    for axis in axes:
        for offset in range(1, lax.axis_size(axis)):
            pl.semaphore_signal(
                barrier, inc=1, device_id={axis: peer_of(axis, offset)}, device_id_type=MESH
            )
            count += 1
    pl.semaphore_wait(barrier, count)


def remote(source, target, send, recv, axis, peer):
    return pltpu.make_async_remote_copy(
        src_ref=source,
        dst_ref=target,
        send_sem=send,
        recv_sem=recv,
        device_id={axis: peer},
        device_id_type=MESH,
    )


def exchange_kernel(axis, gather, block_ref, out_ref, send, recv, own_sem):
    size = lax.axis_size(axis)
    me = lax.axis_index(axis)
    own = pltpu.make_async_copy(
        block_ref if gather else block_ref.at[me], out_ref.at[me], own_sem
    )
    own.start()
    greet((axis,))
    copies = []
    for offset in range(1, size):
        peer = peer_of(axis, offset)
        copy = remote(
            block_ref if gather else block_ref.at[peer],
            out_ref.at[me],
            send.at[offset - 1],
            recv.at[offset - 1],
            axis,
            peer,
        )
        copy.start()
        copies.append(copy)
    own.wait()
    for copy in copies:
        copy.wait()


def exchange(blocks, axis, gather, collective_id):
    size = lax.axis_size(axis)
    shape = (size,) + blocks.shape if gather else blocks.shape
    return pl.pallas_call(
        functools.partial(exchange_kernel, axis, gather),
        out_shape=jax.ShapeDtypeStruct(shape, blocks.dtype),
        in_specs=[pl.BlockSpec(memory_space=pl.ANY)],
        out_specs=pl.BlockSpec(memory_space=pl.ANY),
        scratch_shapes=[
            pltpu.SemaphoreType.DMA((size - 1,)),
            pltpu.SemaphoreType.DMA((size - 1,)),
            pltpu.SemaphoreType.DMA,
        ],
        compiler_params=pltpu.CompilerParams(collective_id=collective_id, has_side_effects=True),
    )(blocks)


def mix_kernel(
    partial_ref,
    residual_ref,
    meta_ref,
    rows_ref,
    all_meta_ref,
    mixed_ref,
    half_slot,
    half_sum,
    part_slot,
    half_send,
    half_recv,
    part_send,
    part_recv,
    row_send,
    row_recv,
    col_send,
    col_recv,
    side_send,
    side_recv,
    meta_send,
    meta_recv,
):
    r, d, t = lax.axis_index("role"), lax.axis_index("dp"), lax.axis_index("tensor")
    dps, tensors = lax.axis_size("dp"), lax.axis_size("tensor")
    group = mixed_ref.shape[0]
    half = tensors * group
    other = 1 - r
    greet(("role", "tensor", "dp"))

    def rows(role, first, count=group):
        return pl.ds(pl.multiple_of(role * half + first * group, group), count)

    halves = remote(
        partial_ref.at[rows(other, 0, half)], half_slot, half_send, half_recv, "role", other
    )
    halves.start()
    all_meta_ref[rows(r, t)] = meta_ref[...]
    metas = []
    for j in range(1, tensors):
        copy = remote(
            meta_ref,
            all_meta_ref.at[rows(r, t)],
            meta_send.at[j],
            meta_recv.at[j],
            "tensor",
            peer_of("tensor", j),
        )
        copy.start()
        metas.append(copy)
    halves.wait()
    half_sum[...] = (
        partial_ref[rows(r, 0, half)].astype(jnp.float32) + half_slot[...].astype(jnp.float32)
    ).astype(jnp.bfloat16)
    parts = []
    for j in range(1, tensors):
        peer = peer_of("tensor", j)
        copy = remote(
            half_sum.at[pl.ds(pl.multiple_of(peer * group, group), group)],
            part_slot.at[j - 1],
            part_send.at[j - 1],
            part_recv.at[j - 1],
            "tensor",
            peer,
        )
        copy.start()
        parts.append(copy)
    for copy in metas:
        copy.wait()
    side_meta = remote(
        all_meta_ref.at[rows(r, 0, half)],
        all_meta_ref.at[rows(r, 0, half)],
        meta_send.at[0],
        meta_recv.at[0],
        "role",
        other,
    )
    side_meta.start()
    total = residual_ref[...].astype(jnp.float32) + half_sum[
        pl.ds(pl.multiple_of(t * group, group), group)
    ].astype(jnp.float32)
    for j in range(1, tensors):
        parts[j - 1].wait()
        total = total + part_slot[j - 1].astype(jnp.float32)
    mixed = total.astype(jnp.bfloat16)
    mixed_ref[...] = mixed
    rows_ref[d, rows(r, t)] = mixed
    along, across, sides = [], {}, []
    for j in range(1, tensors):
        copy = remote(
            mixed_ref,
            rows_ref.at[d, rows(r, t)],
            row_send.at[j - 1],
            row_recv.at[j - 1],
            "tensor",
            peer_of("tensor", j),
        )
        copy.start()
        along.append(copy)
    for j in range(tensors):
        if j > 0:
            along[j - 1].wait()
        block = rows_ref.at[d, rows(r, source_of("tensor", j))]
        for k in range(1, dps):
            copy = remote(
                block, block, col_send.at[k - 1, j], col_recv.at[k - 1, j], "dp", peer_of("dp", k)
            )
            copy.start()
            across[k, j] = copy
    for k in range(dps):
        for j in range(tensors if k > 0 else 0):
            across[k, j].wait()
        block = rows_ref.at[source_of("dp", k), rows(r, 0, half)]
        copy = remote(block, block, side_send.at[k], side_recv.at[k], "role", other)
        copy.start()
        sides.append(copy)
    side_meta.wait()
    for copy in sides:
        copy.wait()


def mix_rows(partial, residual, meta):
    dps, tensors = lax.axis_size("dp"), lax.axis_size("tensor")
    group, width = residual.shape
    tokens = partial.shape[0]
    half = tokens // 2
    vmem = pl.BlockSpec(memory_space=pltpu.VMEM)
    dma = pltpu.SemaphoreType.DMA
    return pl.pallas_call(
        mix_kernel,
        out_shape=[
            jax.ShapeDtypeStruct((dps, tokens, width), jnp.bfloat16),
            jax.ShapeDtypeStruct((tokens, meta.shape[1]), jnp.float32),
            jax.ShapeDtypeStruct((group, width), jnp.bfloat16),
        ],
        in_specs=[vmem] * 3,
        out_specs=[vmem] * 3,
        scratch_shapes=[
            pltpu.VMEM((half, width), jnp.bfloat16),
            pltpu.VMEM((half, width), jnp.bfloat16),
            pltpu.VMEM((tensors - 1, group, width), jnp.bfloat16),
            dma,
            dma,
            dma((tensors - 1,)),
            dma((tensors - 1,)),
            dma((tensors - 1,)),
            dma((tensors - 1,)),
            dma((dps - 1, tensors)),
            dma((dps - 1, tensors)),
            dma((dps,)),
            dma((dps,)),
            dma((tensors,)),
            dma((tensors,)),
        ],
        compiler_params=pltpu.CompilerParams(
            collective_id=2, has_side_effects=True, vmem_limit_bytes=VMEM_BYTES
        ),
    )(partial, residual, meta)


def reduce_kernel(
    partial_ref,
    mixed_ref,
    out_ref,
    side_slot,
    side_sum,
    col_slot,
    half_sum,
    part_slot,
    side_send,
    side_recv,
    col_send,
    col_recv,
    part_send,
    part_recv,
):
    r, t = lax.axis_index("role"), lax.axis_index("tensor")
    dps, tensors = lax.axis_size("dp"), lax.axis_size("tensor")
    group = mixed_ref.shape[0]
    half = tensors * group
    other = 1 - r
    greet(("role", "tensor", "dp"))
    mine = pl.ds(pl.multiple_of(r * half, group), half)
    theirs = pl.ds(pl.multiple_of(other * half, group), half)
    order = [*range(1, dps), 0]
    sides, cols = {}, []
    for k in order:
        copy = remote(
            partial_ref.at[peer_of("dp", k), theirs],
            side_slot.at[k],
            side_send.at[k],
            side_recv.at[k],
            "role",
            other,
        )
        copy.start()
        sides[k] = copy
    for k in order:
        sides[k].wait()
        total = partial_ref[peer_of("dp", k), mine].astype(jnp.float32) + side_slot[k].astype(
            jnp.float32
        )
        if k > 0:
            side_sum[k - 1] = total.astype(jnp.bfloat16)
            copy = remote(
                side_sum.at[k - 1],
                col_slot.at[k - 1],
                col_send.at[k - 1],
                col_recv.at[k - 1],
                "dp",
                peer_of("dp", k),
            )
            copy.start()
            cols.append(copy)
        else:
            half_sum[...] = total
    for k in range(1, dps):
        cols[k - 1].wait()
        half_sum[...] += col_slot[k - 1].astype(jnp.float32)
    side_sum[dps - 1] = half_sum[...].astype(jnp.bfloat16)
    parts = []
    for j in range(1, tensors):
        peer = peer_of("tensor", j)
        copy = remote(
            side_sum.at[dps - 1, pl.ds(pl.multiple_of(peer * group, group), group)],
            part_slot.at[j - 1],
            part_send.at[j - 1],
            part_recv.at[j - 1],
            "tensor",
            peer,
        )
        copy.start()
        parts.append(copy)
    total = (
        mixed_ref[...].astype(jnp.float32) + half_sum[pl.ds(pl.multiple_of(t * group, group), group)]
    )
    for j in range(1, tensors):
        parts[j - 1].wait()
        total = total + part_slot[j - 1].astype(jnp.float32)
    out_ref[...] = total.astype(jnp.bfloat16)


def reduce_rows(partial, mixed_in):
    dps, tensors = lax.axis_size("dp"), lax.axis_size("tensor")
    group, width = mixed_in.shape
    half = tensors * group
    vmem = pl.BlockSpec(memory_space=pltpu.VMEM)
    dma = pltpu.SemaphoreType.DMA
    return pl.pallas_call(
        reduce_kernel,
        out_shape=jax.ShapeDtypeStruct((group, width), jnp.bfloat16),
        in_specs=[vmem] * 2,
        out_specs=vmem,
        scratch_shapes=[
            pltpu.VMEM((dps, half, width), jnp.bfloat16),
            pltpu.VMEM((dps, half, width), jnp.bfloat16),
            pltpu.VMEM((dps - 1, half, width), jnp.bfloat16),
            pltpu.VMEM((half, width), jnp.float32),
            pltpu.VMEM((tensors - 1, group, width), jnp.bfloat16),
            dma((dps,)),
            dma((dps,)),
            dma((dps - 1,)),
            dma((dps - 1,)),
            dma((tensors - 1,)),
            dma((tensors - 1,)),
        ],
        compiler_params=pltpu.CompilerParams(
            collective_id=3, has_side_effects=True, vmem_limit_bytes=VMEM_BYTES
        ),
    )(partial, mixed_in)


def hidden_kernel(
    rows_ref,
    gain_ref,
    meta_ref,
    gates_ref,
    gate_w_ref,
    up_w_ref,
    left_ref,
    hidden_ref,
    coef_ref,
    normed,
    gate_acc,
    up_acc,
):
    step = pl.program_id(1)
    dps, tokens, width = rows_ref.shape

    @pl.when((pl.program_id(0) == 0) & (step == 0))
    def _():
        square = jnp.zeros((tokens, 1), jnp.float32)
        for k in range(dps):
            wide = rows_ref[k].astype(jnp.float32)
            square = square + jnp.sum(wide * wide, axis=1, keepdims=True)
        scale = lax.rsqrt(square / (dps * width) + NORM_EPS)
        for k in range(dps):
            wide = rows_ref[k].astype(jnp.float32)
            normed[k] = (wide * scale * gain_ref[k].astype(jnp.float32)).astype(jnp.bfloat16)

    @pl.when(step == 0)
    def _():
        gate_acc[...] = jnp.zeros_like(gate_acc)
        up_acc[...] = jnp.zeros_like(up_acc)

    block = normed[step]
    gate_acc[...] += jnp.dot(block, gate_w_ref[0], preferred_element_type=jnp.float32)
    up_acc[...] += jnp.dot(block, up_w_ref[0], preferred_element_type=jnp.float32)

    @pl.when(step == dps - 1)
    def _():
        gate = gate_acc[...]
        value = gate / (1.0 + jnp.exp(-gate)) * up_acc[...]
        value = jnp.where(gates_ref[0] > 0.0, value * gates_ref[0], 0.0)
        hidden = value.astype(jnp.bfloat16)
        hidden_ref[0] = hidden
        owner = meta_ref[:, EXPERTS : EXPERTS + 1]
        for tenant in range(TEN):
            coef = jnp.dot(hidden, left_ref[tenant, 0], preferred_element_type=jnp.float32)
            coef = jnp.where(owner == tenant, -coef, 0.0)
            coef_ref[tenant, 0] = coef.astype(jnp.bfloat16)


def hidden_rows(rows, gain, meta, gates, gate_w, up_w, left):
    dps, tokens, width = rows.shape
    experts, _, units = gate_w.shape
    rank = left.shape[-1]
    return pl.pallas_call(
        hidden_kernel,
        grid=(experts, dps),
        out_shape=[
            jax.ShapeDtypeStruct((experts, tokens, units), jnp.bfloat16),
            jax.ShapeDtypeStruct((TEN, experts, tokens, rank), jnp.bfloat16),
        ],
        in_specs=[
            pl.BlockSpec((dps, tokens, width), lambda e, k: (0, 0, 0)),
            pl.BlockSpec((dps, 1, width), lambda e, k: (0, 0, 0)),
            pl.BlockSpec(meta.shape, lambda e, k: (0, 0)),
            pl.BlockSpec((1, tokens, 1), lambda e, k: (e, 0, 0)),
            pl.BlockSpec((1, width, units), lambda e, k: (e, k, 0)),
            pl.BlockSpec((1, width, units), lambda e, k: (e, k, 0)),
            pl.BlockSpec((TEN, 1, units, rank), lambda e, k: (0, e, 0, 0)),
        ],
        out_specs=[
            pl.BlockSpec((1, tokens, units), lambda e, k: (e, 0, 0)),
            pl.BlockSpec((TEN, 1, tokens, rank), lambda e, k: (0, e, 0, 0)),
        ],
        scratch_shapes=[
            pltpu.VMEM((dps, tokens, width), jnp.bfloat16),
            pltpu.VMEM((tokens, units), jnp.float32),
            pltpu.VMEM((tokens, units), jnp.float32),
        ],
        compiler_params=pltpu.CompilerParams(vmem_limit_bytes=VMEM_BYTES),
    )(rows, gain, meta, gates, gate_w, up_w, left)


def down_kernel(hidden_ref, coef_ref, down_ref, right_ref, out_ref):
    experts = hidden_ref.shape[0]
    total = None
    for e in range(experts):
        term = jnp.dot(hidden_ref[e], down_ref[e], preferred_element_type=jnp.float32)
        total = term if total is None else total + term
        for tenant in range(TEN):
            total = total + jnp.dot(
                coef_ref[tenant, e], right_ref[tenant, e], preferred_element_type=jnp.float32
            )
    out_ref[...] = total.astype(jnp.bfloat16)


def down_rows(hidden, coef, down, right, dps):
    experts, tokens, units = hidden.shape
    model = down.shape[2]
    rank = coef.shape[-1]
    width = model // dps
    direct = width % 256 == 0
    block = 256
    per = width // block
    shape = (dps, tokens, width) if direct else (tokens, model)
    if direct:
        out_spec = pl.BlockSpec((None, tokens, block), lambda c: (c // per, 0, c % per))
    else:
        out_spec = pl.BlockSpec((tokens, block), lambda c: (0, c))
    out = pl.pallas_call(
        down_kernel,
        grid=(model // block,),
        out_shape=jax.ShapeDtypeStruct(shape, jnp.bfloat16),
        in_specs=[
            pl.BlockSpec((experts, tokens, units), lambda c: (0, 0, 0)),
            pl.BlockSpec((TEN, experts, tokens, rank), lambda c: (0, 0, 0, 0)),
            pl.BlockSpec((experts, units, block), lambda c: (0, 0, c)),
            pl.BlockSpec(
                (TEN, experts, rank, block), lambda c: (0, 0, 0, c)
            ),
        ],
        out_specs=out_spec,
        compiler_params=pltpu.CompilerParams(vmem_limit_bytes=VMEM_BYTES),
    )(hidden, coef, down, right)
    if not direct:
        out = jnp.transpose(out.reshape(tokens, dps, width), (1, 0, 2))
    return out


def local(
    queries,
    latent_cache,
    new_latent,
    cache_lengths,
    value_proj,
    out_proj,
    residual,
    norm_gain,
    routes,
    gate_values,
    tenant_ids,
    expert_gate_weight,
    expert_up_weight,
    expert_down_weight,
    left_delta_factor,
    factor_right,
):
    seq_count, context, width = latent_cache.shape
    local_heads = queries.shape[1]
    paired = queries.reshape(seq_count, 2, local_heads, width)
    scores = (
        jnp.einsum("sqhd,spd->sqhp", paired, latent_cache, preferred_element_type=jnp.float32)
        * SCORE_SCALE
    )
    present = jnp.arange(context, dtype=jnp.int32)[None, :] < cache_lengths[:, None]
    scores = jnp.where(present[:, None, None, :], scores, MASKED)
    fresh_keys = new_latent.reshape(seq_count, 2, width)
    fresh = (
        jnp.einsum("sqhd,skd->sqhk", paired, fresh_keys, preferred_element_type=jnp.float32)
        * SCORE_SCALE
    )
    causal = jnp.arange(2)[:, None] >= jnp.arange(2)[None, :]
    fresh = jnp.where(causal[None, :, None, :], fresh, MASKED)
    top = jnp.maximum(jnp.max(scores, axis=3), jnp.max(fresh, axis=3))[..., None]
    weights = jnp.exp(scores - top)
    fresh_weights = jnp.exp(fresh - top)
    total = jnp.sum(weights, axis=3) + jnp.sum(fresh_weights, axis=3)
    summed = jnp.einsum(
        "sqhp,spd->sqhd",
        weights.astype(jnp.bfloat16),
        latent_cache[:, :, :LAT],
        preferred_element_type=jnp.float32,
    )
    summed = summed + jnp.einsum(
        "sqhk,skd->sqhd",
        fresh_weights.astype(jnp.bfloat16),
        fresh_keys[:, :, :LAT],
        preferred_element_type=jnp.float32,
    )
    attended = (
        (summed / total[..., None]).astype(jnp.bfloat16).reshape(seq_count * 2, local_heads, LAT)
    )
    dps, tensors = lax.axis_size("dp"), lax.axis_size("tensor")
    own_heads = local_heads // tensors
    blocks = jnp.transpose(
        attended.reshape(seq_count * 2, tensors, own_heads, LAT), (1, 0, 2, 3)
    ).reshape(tensors, seq_count * 2 * own_heads, LAT)
    by_head = exchange(blocks, "tensor", False, 0).reshape(
        tensors * seq_count * 2, own_heads, LAT
    )
    head_values = jnp.einsum(
        "thl,hlv->thv", by_head, value_proj, preferred_element_type=jnp.float32
    ).astype(jnp.bfloat16)
    head_values = head_values.reshape(by_head.shape[0], -1)
    all_values = exchange(head_values, "dp", True, 1).reshape(-1, head_values.shape[1])
    partial = jnp.dot(all_values, out_proj, preferred_element_type=jnp.float32).astype(jnp.bfloat16)
    chosen = routes[:, :, None] == jnp.arange(EXPERTS, dtype=jnp.int32)[None, None, :]
    gate_of = jnp.sum(jnp.where(chosen, gate_values[:, :, None], 0.0), axis=1)
    meta = jnp.concatenate([gate_of, tenant_ids[:, None].astype(jnp.float32)], axis=1)
    meta = jnp.pad(meta, ((0, 0), (0, 128 - meta.shape[1])))
    rows, all_meta, mixed_in = mix_rows(partial, residual, meta)
    local_experts = EXPERTS // dps
    expert_start = lax.axis_index("dp") * local_experts
    own_gates = lax.dynamic_slice_in_dim(all_meta, expert_start, local_experts, 1).T[:, :, None]
    hidden, coef = hidden_rows(
        rows,
        norm_gain.reshape(dps, 1, -1),
        all_meta,
        own_gates,
        expert_gate_weight,
        expert_up_weight,
        left_delta_factor,
    )
    experts_part = down_rows(hidden, coef, expert_down_weight, factor_right, dps)
    return reduce_rows(experts_part, mixed_in)


def solution(mesh):
    placed = (
        P(("dp", "tensor"), "role", None),
        P(("dp", "tensor"), None, None),
        P(("dp", "tensor"), None),
        P(("dp", "tensor")),
        P(("role", "tensor"), None, None),
        P(("role", "tensor"), "dp"),
        P(("role", "tensor"), "dp"),
        P(),
        P(("role", "tensor"), None),
        P(("role", "tensor"), None),
        P(("role", "tensor")),
        P("dp", None, ("role", "tensor")),
        P("dp", None, ("role", "tensor")),
        P("dp", ("role", "tensor"), None),
        P(None, "dp", ("role", "tensor"), None),
        P(None, "dp", None, None),
    )
    return jax.shard_map(
        local, mesh=mesh, in_specs=placed, out_specs=P(("role", "tensor"), "dp"), check_vma=False
    )
```

time: 591 us -> 155 us (0.26)
  blocking collectives: 419 us -> 0 us
  Pallas kernels: 0 us -> 124 us
  waiting for transfers between devices: 84.4 us -> 0 us
  matrix products: 49.8 us -> 18.7 us
  between operations: 14.1 us -> 0.19 us
  local copies, waits for them, and re-layouts: 18.6 us -> 7.65 us
    unnamed x1 -> x0, blocking collectives: 357 us -> none
    pallas_call x0 -> x6, Pallas kernels: none -> 124 us  [the longest x1 30.5 us: mix_rows(): pl.pallas_call(mix_kernel, out_shape=[jax.ShapeDtypeStruct((dps, tokens,...]
    reduce_scatter x2 -> x0, waiting for transfers between devices: 59.6 us -> none  [the longest x1 33 us: local(): lax.psum_scatter(jnp.dot(input_rows, out_proj, preferred_element_type=jnp...]
    all_gather x3 -> x0, blocking collectives: 41.2 us -> none  [the longest x1 22.2 us: local(): lax.all_gather(slot_owner, ('role', 'tensor'), axis=1, tiled=True)]
    dot_general x8 -> x1, matrix products: 41.8 us -> 5.21 us  [local(): jnp.dot(all_values, out_proj, preferred_element_type=jnp.float32)]
    all_gather x1 -> x0, waiting for transfers between devices: 24.8 us -> none  [local(): lax.all_gather(slot_rows, ('role', 'tensor'), axis=1, tiled=True)]
    all_to_all x1 -> x0, blocking collectives: 20.6 us -> none  [local(): lax.all_to_all(attended, 'tensor', split_axis=1, concat_axis=0, tiled=True)]
    sub x2 -> x0, local copies, waits for them, and re-layouts: 13.1 us -> none  [the longest x1 13 us: local(): base_output - jnp.einsum('okei,eoiw->kow', mixing_coefficient, widened_ri...]
  transfers between devices with their start and end apart: 3 -> 0, of which waited for: 3 -> 0; matrix products, arithmetic and copies ran while one was open for 0% -> 0% of each run, Pallas kernels for 0% -> 0%
where the time goes in v2:
time: 155 us; the launch traced here: 154 us
  Pallas kernels  124 us (80%)
  matrix products  18.7 us (12%)
  local copies, waits for them, and re-layouts  7.65 us (5%)
  other arithmetic  4.02 us (3%)
    pallas_call x1, Pallas kernels, mix_rows(): pl.pallas_call(mix_kernel, out_shape=[jax.ShapeDtypeStruct((dps, tokens,...  30.5 us
    pallas_call x1, Pallas kernels, down_rows(): pl.pallas_call(down_kernel, grid=(model // block,), out_shape=jax.ShapeDt...  25.1 us
    pallas_call x2, Pallas kernels, exchange(): pl.pallas_call(functools.partial(exchange_kernel, axis, gather), out_shap...  24.3 us
    pallas_call x1, Pallas kernels, reduce_rows(): pl.pallas_call(reduce_kernel, out_shape=jax.ShapeDtypeStruct((group, widt...  23.6 us
    pallas_call x1, Pallas kernels, hidden_rows(): pl.pallas_call(hidden_kernel, grid=(experts, dps), out_shape=[jax.ShapeDt...  19.9 us
    dot_general x1, matrix products, local(): jnp.dot(all_values, out_proj, preferred_element_type=jnp.float32)  5.21 us
    dot_general x1, matrix products, local(): jnp.einsum('sqhd,spd->sqhp', paired, latent_cache, preferred_element_type...  5.08 us
    dot_general x1, matrix products, local(): jnp.einsum('sqhp,spd->sqhd', weights.astype(jnp.bfloat16), latent_cache[:...  4.75 us

profile of v2, /device:TPU:0, one launch (start us, length us, event | category | flops | bytes accessed | tf_op | source)
XLA Modules:
  0.0 154.1 jit_solution(1825556586146822210)
XLA Ops:
  0.0 0.0 copy-start
  0.0 0.9 iota_compare_fusion.1
  0.9 0.0 copy-start.5
  0.9 0.0 copy-start.3
  0.9 5.1 %fusion.5 = (f32[4,2,64]{2,1,0:T(2,128)S(1)}, f32[4,2,64,1024]{3,2,1,0:T(8,128)}) fusion(pred[4,1024]{1,0:T(4,128)(4,1)S(1)} %iota_compare_fusion.1, bf16[4,2,64,576]{3,2,1,0:T(8,128)(2,1)} %bitcast.50, bf16[4,1024,576]{1,2,0:T(8,128)(2,1)} %param.17), kind=kOutput, calls=%fused_computation.8 | convolution fusion | flops 605552128 | bytes 7411712 | tf_op jit(solution)/shard_map/sqhd,spd->sqhp/dot_general | solution.py:523
  6.0 0.0 copy-done.5
  6.0 0.0 copy-start.2
  6.0 0.0 copy-done.3
  6.0 0.4 fusion.25
  6.5 2.3 %fusion.6 = f32[4,2,64]{2,1,0:T(2,128)S(1)} fusion(f32[4,2,64,1024]{3,2,1,0:T(8,128)} %get-tuple-element.16, f32[4,2,64]{2,1,0:T(2,128)S(1)} %max.7, pred[4,1024]{1,0:T(4,128)(4,1)S(1)} %iota_compare_fusion.1), kind=kLoop, calls=%fused_computation.9 | loop fusion | flops 2096640 | bytes 2105344 | tf_op jit(solution)/shard_map/reduce_sum | solution.py:538
  8.8 0.0 copy-done.2
  8.8 4.7 %fusion.2 = f32[4,2,64,512]{3,2,1,0:T(8,128)} fusion(bf16[4,1024,576]{1,2,0:T(8,128)(2,1)} %param.17, f32[4,2,64,1024]{3,2,1,0:T(8,128)S(1)} %copy-done.2, f32[4,2,64]{2,1,0:T(2,128)S(1)} %max.7, pred[4,1024]{1,0:T(4,128)(4,1)S(1)} %iota_compare_fusion.1), kind=kOutput, calls=%fused_computation.2 | convolution fusion | flops 538968064 | bytes 7346176 | tf_op jit(solution)/shard_map/sqhp,spd->sqhd/dot_general | solution.py:539
  13.6 1.6 %fusion.9 = bf16[4,2,64,512]{3,2,1,0:T(8,128)(2,1)S(1)} fusion(f32[4,2,64,512]{3,2,1,0:T(8,128)} %fusion.2, f32[4,2,64]{2,1,0:T(2,128)S(1)} %add.16, bf16[4,2,576]{2,1,0:T(2,128)(2,1)S(1)} %reshape.64, f32[4,2,64,2]{2,3,1,0:T(2,128)S(1)} %get-tuple-element.18, f32[4,2,64]{2,1,0:T(2,128)S(1)} %max.7), kind=kOutput, calls=%fused_computation.13 | convolution fusion | flops 1837056 | bytes 1597440 | tf_op jit(solution)/shard_map/sqhk,skd->sqhd/dot_general | solution.py:545
  15.2 0.8 copy.38
  16.0 14.8 %shard_map.154 = bf16[4,128,512]{2,1,0:T(8,128)(2,1)} custom-call(bf16[4,128,512]{2,1,0:T(8,128)(2,1)} %bitcast.48), custom_call_target="tpu_custom_call" | custom-call | tf_op jit(solution)/shard_map/pallas_call | solution.py:85
  30.8 0.0 copy-done
  30.9 1.6 %fusion.10 = bf16[16,4,8,128]{3,2,1,0:T(8,128)(2,1)S(1)} fusion(bf16[16,512,128]{2,1,0:T(8,128)(2,1)S(1)} %copy-done, bf16[32,16,512]{2,1,0:T(8,128)(2,1)} %bitcast.49), kind=kOutput, calls=%fused_computation.15 | convolution fusion | flops 67174400 | bytes 2752512 | tf_op jit(solution)/shard_map/thl,hlv->thv/dot_general | solution.py:562
  32.5 0.7 copy.59
  33.2 9.5 %shard_map.155 = bf16[4,32,2048]{2,1,0:T(8,128)(2,1)} custom-call(bf16[32,2048]{1,0:T(8,128)(2,1)} %bitcast.52), custom_call_target="tpu_custom_call" | custom-call | tf_op jit(solution)/shard_map/pallas_call | solution.py:85
  42.7 0.0 copy-start.7
  42.7 0.0 copy-start.8
  42.7 0.0 copy-start.9
  42.7 0.0 copy-start.4
  42.8 5.2 %convolution_convert_fusion.partial_ref = bf16[128,1792]{1,0:T(8,128)(2,1)} fusion(bf16[128,2048]{1,0:T(8,128)(2,1)} %bitcast.47, bf16[2048,1792]{1,0:T(8,128)(2,1)} %param.21), kind=kOutput, calls=%fused_computation.5 | convolution fusion | flops 939753472 | bytes 8323072 | tf_op jit(solution)/shard_map/dot_general | solution.py:567
  48.0 0.0 copy-done.7
  48.0 0.0 copy-start.6
  48.0 0.1 copy.41
  48.0 0.0 copy-done.8
  48.0 0.1 copy.42
  48.1 0.1 select_reduce_fusion
  48.2 0.0 copy-done.9
  48.2 0.1 copy.43
  48.3 0.7 select_maximum_fusion.meta_ref
  49.0 30.5 %shard_map.156 = (bf16[4,128,1792]{2,1,0:T(8,128)(2,1)}, f32[128,128]{1,0:T(8,128)}, bf16[16,1792]{1,0:T(8,128)(2,1)}) custom-call(bf16[128,1792]{1,0:T(8,128)(2,1)} %convolution_convert_fusion.partial_ref, bf16[16,1792]{1,0:T(8,128)(2,1)} %residual_ref.1, f32[16,128]{1,0:T(8,128)} %select_maximum_fusion.meta_ref), custom_call_target="tpu_custom_call" | custom-call | tf_op jit(solution)/shard_map/pallas_call | solution.py:227
  79.6 0.9 dynamic-slice_bitcast_fusion
  80.5 1.7 %copy.46.gates_ref = f32[4,128,1]{2,1,0:T(8,128)} copy(f32[4,128,1]{0,1,2:T(8,128)S(1)} %dynamic-slice_bitcast_fusion) | data formatting | bytes 4096 | tf_op jit(solution)/shard_map/broadcast_in_dim | solution.py:575
  82.2 0.0 copy-done.4
  82.2 1.2 copy.47.left_ref
  83.3 0.0 copy-done.6
  83.3 0.6 reshape.75.gain_ref
  84.0 19.9 %shard_map.157 = (bf16[4,128,256]{2,1,0:T(8,128)(2,1)}, bf16[3,4,128,64]{3,2,1,0:T(8,128)(2,1)}) custom-call(bf16[4,128,1792]{2,1,0:T(8,128)(2,1)} %get-tuple-element.10.rows_ref, bf16[4,1,1792]{2,1,0:T(2,128)(2,1)} %reshape.75.gain_ref, f32[128,128]{1,0:T(8,128)} %get-tuple-element.11.meta_ref, f32[4,128,1]{2,1,0:T(8,128)} %copy.46.gates_ref, ...), custom_call_target="tpu_custom_call" | custom-call | tf_op jit(solution)/shard_map/pallas_call | solution.py:426
  103.9 0.0 copy-start.1
  103.9 25.1 %shard_map.158.partial_ref = bf16[4,128,1792]{2,1,0:T(8,128)(2,1)} custom-call(bf16[4,128,256]{2,1,0:T(8,128)(2,1)} %get-tuple-element.12.hidden_ref, bf16[3,4,128,64]{3,2,1,0:T(8,128)(2,1)} %get-tuple-element.13.coef_ref, bf16[4,256,7168]{2,1,0:T(8,128)(2,1)} %down_ref.1, bf16[3,4,64,7168]{3,2,1,0:T(8,128)(2,1)} %right_ref.1), custom_call_target="tpu_custom_call" | custom-call | tf_op jit(solution)/shard_map/pallas_call | solution.py:481
  129.0 23.6 %shard_map.159 = bf16[16,1792]{1,0:T(8,128)(2,1)} custom-call(bf16[4,128,1792]{2,1,0:T(8,128)(2,1)} %shard_map.158.partial_ref, bf16[16,1792]{1,0:T(8,128)(2,1)} %get-tuple-element.14.mixed_ref), custom_call_target="tpu_custom_call" | custom-call | tf_op jit(solution)/shard_map/pallas_call | solution.py:347
  152.6 1.4 copy.61
  154.1 0.0 copy-done.1
  (7 shorter events, 0.1 us)
Async XLA Ops:
  0.0 30.8 %copy-start = (bf16[16,512,128]{2,1,0:T(8,128)(2,1)S(1)}, bf16[16,512,128]{2,1,0:T(8,128)(2,1)}, u32[]{:S(2)}) copy-start(bf16[16,512,128]{2,1,0:T(8,128)(2,1)} %param.20) | copy-start | bytes 6291460
  0.9 5.1 %copy-start.5 = (bf16[8,576]{1,0:T(8,128)(2,1)S(1)}, bf16[8,576]{1,0:T(8,128)(2,1)}, u32[]{:S(2)}) copy-start(bf16[8,576]{1,0:T(8,128)(2,1)} %param.18) | copy-start | bytes 27652
  0.9 5.1 %copy-start.3 = (bf16[8,64,576]{2,1,0:T(8,128)(2,1)S(1)}, bf16[8,64,576]{2,1,0:T(8,128)(2,1)}, u32[]{:S(2)}) copy-start(bf16[8,64,576]{2,1,0:T(8,128)(2,1)} %param.16) | copy-start | bytes 1769476
  6.0 2.8 %copy-start.2 = (f32[4,2,64,1024]{3,2,1,0:T(8,128)S(1)}, f32[4,2,64,1024]{3,2,1,0:T(8,128)}, u32[]{:S(2)}) copy-start(f32[4,2,64,1024]{3,2,1,0:T(8,128)} %get-tuple-element.16) | copy-start | bytes 6291460
  42.7 5.3 %copy-start.7 = (s32[16,8]{0,1:T(8,128)S(1)}, s32[16,8]{0,1:T(8,128)}, u32[]{:S(2)}) copy-start(s32[16,8]{0,1:T(8,128)} %param.24) | copy-start | bytes 1540
  42.7 5.3 %copy-start.8 = (f32[16,8]{0,1:T(8,128)S(1)}, f32[16,8]{0,1:T(8,128)}, u32[]{:S(2)}) copy-start(f32[16,8]{0,1:T(8,128)} %param.25) | copy-start | bytes 1540
  42.7 5.5 %copy-start.9 = (s32[16]{0:T(128)S(1)}, s32[16]{0:T(128)}, u32[]{:S(2)}) copy-start(s32[16]{0:T(128)} %param.26) | copy-start | bytes 196
  42.7 39.4 %copy-start.4 = (bf16[3,4,256,64]{2,3,1,0:T(8,128)(2,1)S(1)}, bf16[3,4,256,64]{2,3,1,0:T(8,128)(2,1)}, u32[]{:S(2)}) copy-start(bf16[3,4,256,64]{2,3,1,0:T(8,128)(2,1)} %param.30) | copy-start | bytes 1179652
  48.0 35.4 %copy-start.6 = (bf16[7168]{0:T(1024)(128)(2,1)S(1)}, bf16[7168]{0:T(1024)(128)(2,1)}, u32[]{:S(2)}) copy-start(bf16[7168]{0:T(1024)(128)(2,1)} %param.23) | copy-start | bytes 43012
  103.9 50.2 %copy-start.1 = (bf16[16,512,128]{2,1,0:T(8,128)(2,1)S(1)}, bf16[16,512,128]{2,1,0:T(8,128)(2,1)}, u32[]{:S(2)}) copy-start(bf16[16,512,128]{2,1,0:T(8,128)(2,1)} %param.20) | copy-start | bytes 6291460

commit v3 on v2

--- a/solution.py
+++ b/solution.py
@@ -50,6 +50,100 @@
         recv_sem=recv,
         device_id={axis: peer},
         device_id_type=MESH,
+    )
+
+
+def attend_kernel(
+    lengths_ref, query_ref, cache_ref, fresh_ref, out_ref, keys_ref, stage, load, send, recv
+):
+    heads, width = query_ref.shape[1:]
+    tensors, seqs, _, own_heads, _ = out_ref.shape
+    loads = []
+    for s in range(seqs):
+        copy = pltpu.make_async_copy(cache_ref.at[s], keys_ref.at[s], load.at[s])
+        copy.start()
+        loads.append(copy)
+    greet(("tensor",))
+    me = lax.axis_index("tensor")
+    copies = []
+    for s in range(seqs):
+        query = query_ref[2 * s : 2 * s + 2].reshape(2 * heads, width)
+        loads[s].wait()
+        scores = jnp.dot(query, keys_ref[s], preferred_element_type=jnp.float32) * SCORE_SCALE
+        place = lax.broadcasted_iota(jnp.int32, scores.shape, 1)
+        scores = jnp.where(place < lengths_ref[s], scores, MASKED)
+        wide = query.astype(jnp.float32)
+        keys = [fresh_ref[s, i : i + 1].astype(jnp.float32) for i in range(2)]
+        fresh = [jnp.sum(wide * key, axis=1, keepdims=True) * SCORE_SCALE for key in keys]
+        later = lax.broadcasted_iota(jnp.int32, fresh[1].shape, 0) >= heads
+        fresh[1] = jnp.where(later, fresh[1], MASKED)
+        top = jnp.maximum(
+            jnp.max(scores, axis=1, keepdims=True), jnp.maximum(fresh[0], fresh[1])
+        )
+        weights = jnp.exp(scores - top)
+        fresh = [jnp.exp(score - top) for score in fresh]
+        total = jnp.sum(weights, axis=1, keepdims=True) + fresh[0] + fresh[1]
+        summed = lax.dot_general(
+            weights.astype(jnp.bfloat16),
+            keys_ref[s, :LAT],
+            (((1,), (1,)), ((), ())),
+            preferred_element_type=jnp.float32,
+        )
+        for weight, key in zip(fresh, keys):
+            summed = summed + weight.astype(jnp.bfloat16).astype(jnp.float32) * key[:, :LAT]
+        attended = (summed / total).astype(jnp.bfloat16)
+        for step in range(2):
+            for part in range(tensors):
+                first = step * heads + part * own_heads
+                stage[part, s, step] = attended[first : first + own_heads]
+        for j in range(1, tensors):
+            peer = peer_of("tensor", j)
+            copy = remote(
+                stage.at[peer, s],
+                out_ref.at[me, s],
+                send.at[s, j - 1],
+                recv.at[s, j - 1],
+                "tensor",
+                peer,
+            )
+            copy.start()
+            copies.append(copy)
+        out_ref[me, s] = stage[me, s]
+    for copy in copies:
+        copy.wait()
+
+
+def attend(queries, latent_cache, new_latent, cache_lengths, tensors):
+    heads, width = queries.shape[1:]
+    seqs, context, _ = latent_cache.shape
+    own_heads = heads // tensors
+    vmem = pl.BlockSpec(memory_space=pltpu.VMEM)
+    shape = (tensors, seqs, 2, own_heads, LAT)
+    return pl.pallas_call(
+        attend_kernel,
+        out_shape=jax.ShapeDtypeStruct(shape, jnp.bfloat16),
+        in_specs=[
+            pl.BlockSpec(memory_space=pltpu.SMEM),
+            vmem,
+            pl.BlockSpec(memory_space=pl.ANY),
+            vmem,
+        ],
+        out_specs=vmem,
+        scratch_shapes=[
+            pltpu.VMEM((seqs, width, context), jnp.bfloat16),
+            pltpu.VMEM(shape, jnp.bfloat16),
+            pltpu.SemaphoreType.DMA((seqs,)),
+            pltpu.SemaphoreType.DMA((seqs, tensors - 1)),
+            pltpu.SemaphoreType.DMA((seqs, tensors - 1)),
+        ],
+        compiler_params=pltpu.CompilerParams(
+            collective_id=0, has_side_effects=True, vmem_limit_bytes=VMEM_BYTES
+        ),
+    )(
+        cache_lengths,
+        queries,
+        jnp.swapaxes(latent_cache, 1, 2),
+        new_latent.reshape(seqs, 2, width),
     )
 
 
@@ -372,7 +466,6 @@
     rows_ref,
     gain_ref,
     meta_ref,
-    gates_ref,
     gate_w_ref,
     up_w_ref,
     left_ref,
@@ -409,39 +502,41 @@
     def _():
         gate = gate_acc[...]
         value = gate / (1.0 + jnp.exp(-gate)) * up_acc[...]
-        value = jnp.where(gates_ref[0] > 0.0, value * gates_ref[0], 0.0)
+        label = lax.axis_index("dp") * pl.num_programs(0) + pl.program_id(0)
+        lane = lax.broadcasted_iota(jnp.int32, meta_ref.shape, 1)
+        own = jnp.sum(jnp.where(lane == label, meta_ref[...], 0.0), axis=1, keepdims=True)
+        value = jnp.where(own > 0.0, value * own, 0.0)
         hidden = value.astype(jnp.bfloat16)
         hidden_ref[0] = hidden
         owner = meta_ref[:, EXPERTS : EXPERTS + 1]
-        for tenant in range(TEN):
-            coef = jnp.dot(hidden, left_ref[tenant, 0], preferred_element_type=jnp.float32)
-            coef = jnp.where(owner == tenant, -coef, 0.0)
-            coef_ref[tenant, 0] = coef.astype(jnp.bfloat16)
-
-
-def hidden_rows(rows, gain, meta, gates, gate_w, up_w, left):
+        coef = jnp.dot(hidden, left_ref[0], preferred_element_type=jnp.float32)
+        tenant = lax.broadcasted_iota(jnp.int32, coef.shape, 1) // (coef.shape[1] // TEN)
+        coef = jnp.where(owner == tenant.astype(jnp.float32), -coef, 0.0)
+        coef_ref[0] = coef.astype(jnp.bfloat16)
+
+
+def hidden_rows(rows, gain, meta, gate_w, up_w, left):
     dps, tokens, width = rows.shape
     experts, _, units = gate_w.shape
-    rank = left.shape[-1]
+    depth = left.shape[-1]
     return pl.pallas_call(
         hidden_kernel,
         grid=(experts, dps),
         out_shape=[
             jax.ShapeDtypeStruct((experts, tokens, units), jnp.bfloat16),
-            jax.ShapeDtypeStruct((TEN, experts, tokens, rank), jnp.bfloat16),
+            jax.ShapeDtypeStruct((experts, tokens, depth), jnp.bfloat16),
         ],
         in_specs=[
             pl.BlockSpec((dps, tokens, width), lambda e, k: (0, 0, 0)),
             pl.BlockSpec((dps, 1, width), lambda e, k: (0, 0, 0)),
             pl.BlockSpec(meta.shape, lambda e, k: (0, 0)),
-            pl.BlockSpec((1, tokens, 1), lambda e, k: (e, 0, 0)),
             pl.BlockSpec((1, width, units), lambda e, k: (e, k, 0)),
             pl.BlockSpec((1, width, units), lambda e, k: (e, k, 0)),
-            pl.BlockSpec((TEN, 1, units, rank), lambda e, k: (0, e, 0, 0)),
+            pl.BlockSpec((1, units, depth), lambda e, k: (e, 0, 0)),
         ],
         out_specs=[
             pl.BlockSpec((1, tokens, units), lambda e, k: (e, 0, 0)),
-            pl.BlockSpec((TEN, 1, tokens, rank), lambda e, k: (0, e, 0, 0)),
+            pl.BlockSpec((1, tokens, depth), lambda e, k: (e, 0, 0)),
         ],
         scratch_shapes=[
             pltpu.VMEM((dps, tokens, width), jnp.bfloat16),
@@ -449,30 +544,33 @@
             pltpu.VMEM((tokens, units), jnp.float32),
         ],
         compiler_params=pltpu.CompilerParams(vmem_limit_bytes=VMEM_BYTES),
-    )(rows, gain, meta, gates, gate_w, up_w, left)
+    )(rows, gain, meta, gate_w, up_w, left)
 
 
 def down_kernel(hidden_ref, coef_ref, down_ref, right_ref, out_ref):
     experts = hidden_ref.shape[0]
+    depth, block = coef_ref.shape[2], right_ref.shape[3]
     total = None
     for e in range(experts):
         term = jnp.dot(hidden_ref[e], down_ref[e], preferred_element_type=jnp.float32)
         total = term if total is None else total + term
-        for tenant in range(TEN):
-            total = total + jnp.dot(
-                coef_ref[tenant, e], right_ref[tenant, e], preferred_element_type=jnp.float32
-            )
+        total = total + jnp.dot(
+            coef_ref[e],
+            right_ref[:, e].reshape(depth, block),
+            preferred_element_type=jnp.float32,
+        )
     out_ref[...] = total.astype(jnp.bfloat16)
 
 
 def down_rows(hidden, coef, down, right, dps):
     experts, tokens, units = hidden.shape
     model = down.shape[2]
-    rank = coef.shape[-1]
+    depth = coef.shape[-1]
+    rank = right.shape[2]
     width = model // dps
-    direct = width % 256 == 0
-    block = 256
-    per = width // block
+    direct = width % 896 == 0
+    block = 896 if direct else 256
+    per = max(width // block, 1)
     shape = (dps, tokens, width) if direct else (tokens, model)
     if direct:
         out_spec = pl.BlockSpec((None, tokens, block), lambda c: (c // per, 0, c % per))
@@ -484,7 +582,7 @@
         out_shape=jax.ShapeDtypeStruct(shape, jnp.bfloat16),
         in_specs=[
             pl.BlockSpec((experts, tokens, units), lambda c: (0, 0, 0)),
-            pl.BlockSpec((TEN, experts, tokens, rank), lambda c: (0, 0, 0, 0)),
+            pl.BlockSpec((experts, tokens, depth), lambda c: (0, 0, 0)),
             pl.BlockSpec((experts, units, block), lambda c: (0, 0, c)),
             pl.BlockSpec(
                 (TEN, experts, rank, block), lambda c: (0, 0, 0, c)
@@ -516,47 +614,10 @@
     left_delta_factor,
     factor_right,
 ):
-    seq_count, context, width = latent_cache.shape
-    local_heads = queries.shape[1]
-    paired = queries.reshape(seq_count, 2, local_heads, width)
-    scores = (
-        jnp.einsum("sqhd,spd->sqhp", paired, latent_cache, preferred_element_type=jnp.float32)
-        * SCORE_SCALE
-    )
-    present = jnp.arange(context, dtype=jnp.int32)[None, :] < cache_lengths[:, None]
-    scores = jnp.where(present[:, None, None, :], scores, MASKED)
-    fresh_keys = new_latent.reshape(seq_count, 2, width)
-    fresh = (
-        jnp.einsum("sqhd,skd->sqhk", paired, fresh_keys, preferred_element_type=jnp.float32)
-        * SCORE_SCALE
-    )
-    causal = jnp.arange(2)[:, None] >= jnp.arange(2)[None, :]
-    fresh = jnp.where(causal[None, :, None, :], fresh, MASKED)
-    top = jnp.maximum(jnp.max(scores, axis=3), jnp.max(fresh, axis=3))[..., None]
-    weights = jnp.exp(scores - top)
-    fresh_weights = jnp.exp(fresh - top)
-    total = jnp.sum(weights, axis=3) + jnp.sum(fresh_weights, axis=3)
-    summed = jnp.einsum(
-        "sqhp,spd->sqhd",
-        weights.astype(jnp.bfloat16),
-        latent_cache[:, :, :LAT],
-        preferred_element_type=jnp.float32,
-    )
-    summed = summed + jnp.einsum(
-        "sqhk,skd->sqhd",
-        fresh_weights.astype(jnp.bfloat16),
-        fresh_keys[:, :, :LAT],
-        preferred_element_type=jnp.float32,
-    )
-    attended = (
-        (summed / total[..., None]).astype(jnp.bfloat16).reshape(seq_count * 2, local_heads, LAT)
-    )
+    seq_count = latent_cache.shape[0]
     dps, tensors = lax.axis_size("dp"), lax.axis_size("tensor")
-    own_heads = local_heads // tensors
-    blocks = jnp.transpose(
-        attended.reshape(seq_count * 2, tensors, own_heads, LAT), (1, 0, 2, 3)
-    ).reshape(tensors, seq_count * 2 * own_heads, LAT)
-    by_head = exchange(blocks, "tensor", False, 0).reshape(
+    own_heads = queries.shape[1] // tensors
+    by_head = attend(queries, latent_cache, new_latent, cache_lengths, tensors).reshape(
         tensors * seq_count * 2, own_heads, LAT
     )
     head_values = jnp.einsum(
@@ -570,17 +631,15 @@
     meta = jnp.concatenate([gate_of, tenant_ids[:, None].astype(jnp.float32)], axis=1)
     meta = jnp.pad(meta, ((0, 0), (0, 128 - meta.shape[1])))
     rows, all_meta, mixed_in = mix_rows(partial, residual, meta)
-    local_experts = EXPERTS // dps
-    expert_start = lax.axis_index("dp") * local_experts
-    own_gates = lax.dynamic_slice_in_dim(all_meta, expert_start, local_experts, 1).T[:, :, None]
+    left = jnp.transpose(left_delta_factor, (1, 2, 0, 3))
+    left = left.reshape(left.shape[0], left.shape[1], -1)
     hidden, coef = hidden_rows(
         rows,
         norm_gain.reshape(dps, 1, -1),
         all_meta,
-        own_gates,
         expert_gate_weight,
         expert_up_weight,
-        left_delta_factor,
+        left,
     )
     experts_part = down_rows(hidden, coef, expert_down_weight, factor_right, dps)
     return reduce_rows(experts_part, mixed_in)

time: 155 us -> 132 us (0.85)
  matrix products: 18.7 us -> 6.81 us
  Pallas kernels: 124 us -> 115 us
  other arithmetic: 4.02 us -> 1.59 us
    pallas_call x0 -> x1, Pallas kernels: none -> 20.1 us  [attend(): pl.pallas_call(attend_kernel, out_shape=jax.ShapeDtypeStruct(shape, jnp.b...]
    pallas_call x2 -> x1, Pallas kernels: 24.3 us -> 8.48 us  [exchange(): pl.pallas_call(functools.partial(exchange_kernel, axis, gather), out_shap...]
    dot_general x4 -> x0, matrix products: 11.9 us -> none  [the longest x1 5.08 us: local(): jnp.einsum('sqhd,spd->sqhp', paired, latent_cache, preferred_element_type...]
    pallas_call x1, Pallas kernels: 25.1 us -> 13.4 us  [down_rows(): pl.pallas_call(down_kernel, grid=(model // block,), out_shape=jax.ShapeDt...]
    broadcast_in_dim x2 -> x0, local copies, waits for them, and re-layouts: 2.63 us -> none  [local(): lax.dynamic_slice_in_dim(all_meta, expert_start, local_experts, 1)]
    reduce_sum x2 -> x0, other arithmetic: 2.33 us -> none  [local(): total = jnp.sum(weights, axis=3) + jnp.sum(fresh_weights, axis=3)]
    reshape x2, local copies, waits for them, and re-layouts: 0.03 us -> 2.33 us  [the longest x1 1.31 us: attend(): new_latent.reshape(seqs, 2, width)]
    unnamed x24 -> x8, local copies, waits for them, and re-layouts: 2.8 us -> 3.99 us
where the time goes in v3:
time: 132 us
  Pallas kernels  115 us (87%)
  local copies, waits for them, and re-layouts  8.41 us (6%)
  matrix products  6.81 us (5%)
  other arithmetic  1.59 us (1%)
    pallas_call x1, Pallas kernels, mix_rows(): pl.pallas_call(mix_kernel, out_shape=[jax.ShapeDtypeStruct((dps, tokens,...  29.1 us
    pallas_call x1, Pallas kernels, reduce_rows(): pl.pallas_call(reduce_kernel, out_shape=jax.ShapeDtypeStruct((group, widt...  23.7 us
    pallas_call x1, Pallas kernels, attend(): pl.pallas_call(attend_kernel, out_shape=jax.ShapeDtypeStruct(shape, jnp.b...  20.1 us
    pallas_call x1, Pallas kernels, hidden_rows(): pl.pallas_call(hidden_kernel, grid=(experts, dps), out_shape=[jax.ShapeDt...  20 us
    pallas_call x1, Pallas kernels, down_rows(): pl.pallas_call(down_kernel, grid=(model // block,), out_shape=jax.ShapeDt...  13.4 us
    pallas_call x1, Pallas kernels, exchange(): pl.pallas_call(functools.partial(exchange_kernel, axis, gather), out_shap...  8.48 us
    dot_general x1, matrix products, local(): jnp.dot(all_values, out_proj, preferred_element_type=jnp.float32)  5.18 us
    unnamed x8, local copies, waits for them, and re-layouts  3.99 us

profile of v3, /device:TPU:0, one launch (start us, length us, event | category | flops | bytes accessed | tf_op | source)
XLA Modules:
  0.0 131.6 jit_solution(14029390894302934587)
XLA Ops:
  0.0 0.0 copy-start
  0.0 0.8 convert_bitcast_fusion
  0.8 0.1 copy.35
  0.9 0.8 copy.33
  1.7 0.8 copy.34
  2.4 0.1 select_reduce_fusion
  2.5 0.7 select_maximum_fusion.meta_ref
  3.2 1.3 reshape.21.fresh_ref
  4.5 1.3 %reshape.27.gain_ref = bf16[4,1,1792]{2,1,0:T(2,128)(2,1)} reshape(bf16[7168]{0:T(1024)(128)(2,1)} %param.23) | data formatting | bytes 28672 | tf_op jit(solution)/shard_map/reshape | solution.py:638
  5.8 1.0 copy.36
  6.9 1.0 copy.38.left_ref
  7.9 20.1 %shard_map.154 = bf16[4,4,2,16,512]{4,3,2,1,0:T(8,128)(2,1)} custom-call(s32[4]{0:T(128)} %lengths_ref.1, bf16[8,64,576]{2,1,0:T(8,128)(2,1)} %query_ref.1, bf16[4,576,1024]{2,1,0:T(8,128)(2,1)} %bitcast.17, bf16[4,2,576]{2,1,0:T(2,128)(2,1)} %reshape.21.fresh_ref), custom_call_target="tpu_custom_call" | custom-call | tf_op jit(solution)/shard_map/pallas_call | solution.py:122
  28.0 0.0 copy-done
  28.0 1.6 %fusion = bf16[16,4,8,128]{3,2,1,0:T(8,128)(2,1)S(1)} fusion(bf16[16,512,128]{2,1,0:T(8,128)(2,1)S(1)} %copy-done, bf16[32,16,512]{2,1,0:T(8,128)(2,1)} %bitcast.19), kind=kOutput, calls=%fused_computation.2 | convolution fusion | flops 67174400 | bytes 2752512 | tf_op jit(solution)/shard_map/thl,hlv->thv/dot_general | solution.py:623
  29.7 0.7 copy.43
  30.3 8.5 %shard_map.155 = bf16[4,32,2048]{2,1,0:T(8,128)(2,1)} custom-call(bf16[32,2048]{1,0:T(8,128)(2,1)} %bitcast.21), custom_call_target="tpu_custom_call" | custom-call | tf_op jit(solution)/shard_map/pallas_call | solution.py:179
  38.8 5.2 %convolution_convert_fusion.partial_ref = bf16[128,1792]{1,0:T(8,128)(2,1)} fusion(bf16[128,2048]{1,0:T(8,128)(2,1)} %bitcast.18, bf16[2048,1792]{1,0:T(8,128)(2,1)} %param.21), kind=kOutput, calls=%fused_computation | convolution fusion | flops 939753472 | bytes 8323072 | tf_op jit(solution)/shard_map/dot_general | solution.py:628
  44.0 29.1 %shard_map.156 = (bf16[4,128,1792]{2,1,0:T(8,128)(2,1)}, f32[128,128]{1,0:T(8,128)}, bf16[16,1792]{1,0:T(8,128)(2,1)}) custom-call(bf16[128,1792]{1,0:T(8,128)(2,1)} %convolution_convert_fusion.partial_ref, bf16[16,1792]{1,0:T(8,128)(2,1)} %residual_ref.1, f32[16,128]{1,0:T(8,128)} %select_maximum_fusion.meta_ref), custom_call_target="tpu_custom_call" | custom-call | tf_op jit(solution)/shard_map/pallas_call | solution.py:321
  73.1 20.0 %shard_map.157 = (bf16[4,128,256]{2,1,0:T(8,128)(2,1)}, bf16[4,128,192]{2,1,0:T(8,128)(2,1)}) custom-call(bf16[4,128,1792]{2,1,0:T(8,128)(2,1)} %get-tuple-element.10.rows_ref, bf16[4,1,1792]{2,1,0:T(2,128)(2,1)} %reshape.27.gain_ref, f32[128,128]{1,0:T(8,128)} %get-tuple-element.11.meta_ref, bf16[4,7168,256]{2,1,0:T(8,128)(2,1)} %gate_w_ref.1, ...), custom_call_target="tpu_custom_call" | custom-call | tf_op jit(solution)/shard_map/pallas_call | solution.py:522
  93.1 0.0 copy-start.1
  93.1 13.4 %shard_map.158.partial_ref = bf16[4,128,1792]{2,1,0:T(8,128)(2,1)} custom-call(bf16[4,128,256]{2,1,0:T(8,128)(2,1)} %get-tuple-element.12.hidden_ref, bf16[4,128,192]{2,1,0:T(8,128)(2,1)} %get-tuple-element.13.coef_ref, bf16[4,256,7168]{2,1,0:T(8,128)(2,1)} %down_ref.1, bf16[3,4,64,7168]{3,2,1,0:T(8,128)(2,1)} %right_ref.1), custom_call_target="tpu_custom_call" | custom-call | tf_op jit(solution)/shard_map/pallas_call | solution.py:579
  106.5 23.7 %shard_map.159 = bf16[16,1792]{1,0:T(8,128)(2,1)} custom-call(bf16[4,128,1792]{2,1,0:T(8,128)(2,1)} %shard_map.158.partial_ref, bf16[16,1792]{1,0:T(8,128)(2,1)} %get-tuple-element.14.mixed_ref), custom_call_target="tpu_custom_call" | custom-call | tf_op jit(solution)/shard_map/pallas_call | solution.py:441
  130.2 1.4 %copy.45 = bf16[16,1792]{1,0:T(8,128)(2,1)} copy(bf16[16,1792]{1,0:T(8,128)(2,1)} %shard_map.159) | data formatting | bytes 114688
  131.6 0.0 copy-done.1
Async XLA Ops:
  0.0 28.0 %copy-start = (bf16[16,512,128]{2,1,0:T(8,128)(2,1)S(1)}, bf16[16,512,128]{2,1,0:T(8,128)(2,1)}, u32[]{:S(2)}) copy-start(bf16[16,512,128]{2,1,0:T(8,128)(2,1)} %param.20) | copy-start | bytes 6291460
  93.1 38.5 %copy-start.1 = (bf16[16,512,128]{2,1,0:T(8,128)(2,1)S(1)}, bf16[16,512,128]{2,1,0:T(8,128)(2,1)}, u32[]{:S(2)}) copy-start(bf16[16,512,128]{2,1,0:T(8,128)(2,1)} %param.20) | copy-start | bytes 6291460
